TPU v7x, 32 devices: a whole 2x2x4 slice. The times are simulated.
32 devices in a mesh: groups: 2 (over y), expert: 16 (over z, x, core), dp: 1.
Axes of the slice: x: 2, y: 2, z: 4, core: 2. Of those that a mesh axis runs over, the one named last changes fastest.
Arguments:
- cotangent: bfloat16 [4096, 4096], P(('groups', 'expert', 'dp')), parts along dimension 0, may hold values from -6 to 6
- hidden: bfloat16 [4096, 8, 768], P(('groups', 'expert', 'dp')), parts along dimension 0, may hold values from -6 to 6
- gates: bfloat16 [4096, 8], P(('groups', 'expert', 'dp')), parts along dimension 0, may hold values from 0.099609375 to 1
- expert_ids: int32 [4096, 8], P(('groups', 'expert', 'dp')), parts along dimension 0, may hold values from 0 to 15, all different within a row; in each aligned block of 128 rows (0 to 127, 128 to 255, ...) at most 80 rows name the same one
- counts: int32 [32], P(('groups', 'expert', 'dp')), parts along dimension 0, may hold values from 32 to 128
- proj_out: bfloat16 [64, 4096], P(None, 'dp'), may hold values from -0.09375 to 0.09375
- proj_in: bfloat16 [16, 64, 768], P('expert', None, 'dp'), may hold values from -0.21875 to 0.21875
Outputs:
- grads: bfloat16 [32, 16, 4096], P(('groups', 'expert', 'dp')), parts along dimension 0
There are 2 independent parts, one for each index of `groups`. A program takes and returns all parts, laid end to end along the dimension named above; an argument that names none is the same for every part. Nothing has to cross between parts.
Inputs may be any that keep to these rules, and one draw needn't show every extreme that they name: `expert_ids`: each row names 8 different experts. Among the 128 rows of one device, no expert is named more than 80 times, a bound that some block reaches.
All inputs are finite; a program needn't handle non-finite values.
Results may differ from a plain program's by a relative error of at most 0.0057.
Values may be sent and summed in bfloat16 or wider, within the bound.
A program may use at most 64 MiB of HBM per device.

v0:
```python
import jax
import jax.numpy as jnp
from jax import lax
from jax.sharding import PartitionSpec as P


def slot_layout(expert_ids, expert_count, capacity):
    tokens_dev, top_k = expert_ids.shape
    routes = tokens_dev * top_k
    expert_hot = (
        expert_ids[:, :, None] == jnp.arange(expert_count, dtype=jnp.int32)[None, None, :]
    ).astype(jnp.bfloat16)
    per_token = jnp.sum(expert_hot, axis=1)
    token_pos = jnp.arange(tokens_dev, dtype=jnp.int32)
    lower_mask = (token_pos[:, None] > token_pos[None, :]).astype(jnp.bfloat16)
    before = jnp.dot(lower_mask, per_token, preferred_element_type=jnp.float32)
    rank_in = jnp.sum(before[:, None, :] * expert_hot.astype(jnp.float32), axis=2).astype(jnp.int32)
    flat_ids = expert_ids.reshape(routes)
    target = flat_ids * capacity + rank_in.reshape(routes)
    route_of = (
        jnp.zeros((expert_count * capacity,), jnp.int32)
        .at[target]
        .set(jnp.arange(routes, dtype=jnp.int32))
    )
    filled = (
        jnp.zeros((expert_count * capacity,), jnp.bfloat16)
        .at[target]
        .set(jnp.ones((routes,), jnp.bfloat16))
    )
    return (route_of, filled)


def outer_sums(scaled_slots, reduced_slots):
    return jnp.einsum(
        "sjxi,sjk->xsik", scaled_slots, reduced_slots, preferred_element_type=jnp.float32
    ).astype(jnp.bfloat16)


def on_device(cotangent, hidden, gates, expert_ids, counts, proj_out, proj_in):
    tokens_dev, top_k = expert_ids.shape
    examples = counts.shape[0]
    seq_len = tokens_dev // examples
    hidden_width = hidden.shape[2]
    rank_dim = proj_out.shape[0]
    expert_count = lax.axis_size("expert")
    capacity = min(tokens_dev, max(2, 5 * tokens_dev * top_k // (4 * expert_count)))
    slots = expert_count * capacity
    routes = tokens_dev * top_k
    basis_out, basis_in = (
        lax.all_gather(proj_out, "dp", axis=1, tiled=True),
        lax.all_gather(proj_in[0], "dp", axis=1, tiled=True),
    )
    position = jnp.arange(tokens_dev, dtype=jnp.int32)
    example_of = position // seq_len
    live_mask = (position % seq_len < counts[example_of]).astype(jnp.bfloat16)
    member = (example_of[:, None] == jnp.arange(examples, dtype=jnp.int32)[None, :]).astype(
        jnp.bfloat16
    )
    route_weights = (gates * live_mask[:, None])[:, :, None] * member[:, None, :]
    route_of, filled = slot_layout(expert_ids, expert_count, capacity)
    hidden_slots = hidden.reshape(routes, hidden_width)[route_of]
    projected = jnp.dot(cotangent, basis_out.T, preferred_element_type=jnp.float32)
    scaled = (
        route_weights.astype(jnp.float32)[:, :, :, None] * projected[:, None, None, :]
    ).astype(jnp.bfloat16)
    scaled_slots = scaled.reshape(routes, examples * rank_dim)[route_of] * filled[:, None]
    recv_scaled, recv_hidden = (
        lax.all_to_all(
            scaled_slots.reshape(expert_count, capacity * examples * rank_dim),
            "expert",
            split_axis=0,
            concat_axis=0,
            tiled=True,
        ),
        lax.all_to_all(
            hidden_slots.reshape(expert_count, capacity * hidden_width),
            "expert",
            split_axis=0,
            concat_axis=0,
            tiled=True,
        ),
    )
    reduced = jnp.dot(
        recv_hidden.reshape(slots, hidden_width), basis_in.T, preferred_element_type=jnp.float32
    ).astype(jnp.bfloat16)
    blocks = outer_sums(
        recv_scaled.reshape(expert_count, capacity, examples, rank_dim),
        reduced.reshape(expert_count, capacity, rank_dim),
    )
    grads = lax.all_to_all(
        blocks.reshape(examples, expert_count, rank_dim * rank_dim),
        "expert",
        split_axis=1,
        concat_axis=1,
        tiled=True,
    )
    return grads


def solution(mesh):
    placed = (
        P(("groups", "expert", "dp"), None),
        P(("groups", "expert", "dp"), None, None),
        P(("groups", "expert", "dp"), None),
        P(("groups", "expert", "dp"), None),
        P(("groups", "expert", "dp")),
        P(None, "dp"),
        P("expert", None, "dp"),
    )
    return jax.shard_map(
        on_device,
        mesh=mesh,
        in_specs=placed,
        out_specs=P(("groups", "expert", "dp"), None, None),
        check_vma=False,
    )
```

profile of v0, /device:TPU:0, one launch (start us, length us, event | category | flops | bytes accessed | tf_op | source)
XLA Modules:
  0.0 146.1 jit_solution(15648535779732791456)
XLA Ops:
  1.6 0.7 multiply_reduce_fusion
  3.3 4.3 %scatter_custom_fusion = s32[1280]{0:T(1024)S(1)} fusion(s32[1024]{0:T(1024)S(1)} %bitcast.31, s32[1024]{0:T(1024)S(1)} %iota.25, s32[]{:T(128)} %constant.37.clone.1), kind=kCustom, calls=%fused_computation.21 | custom fusion | bytes 5124 | tf_op jit(solution)/shard_map/scatter | solution.py:23
  7.6 7.6 %scatter_custom_fusion.1 = bf16[1280]{0:T(1024)(128)(2,1)S(1)} fusion(s32[1024]{0:T(1024)S(1)} %bitcast.32, bf16[1024]{0:T(1024)(128)(2,1)S(1)} %broadcast.124, bf16[]{:T(256)} %constant.39.clone.1), kind=kCustom, calls=%fused_computation.23 | custom fusion | bytes 2562 | tf_op jit(solution)/shard_map/scatter | solution.py:28
  16.2 1.8 %fusion.11 = f32[128,64]{1,0:T(8,128)S(1)} fusion(bf16[128,4096]{1,0:T(8,128)(2,1)} %param.7, bf16[64,4096]{1,0:T(8,128)(2,1)} %param.12), kind=kOutput, calls=%fused_computation.33 | convolution fusion | flops 67108864 | bytes 1605632 | tf_op jit(solution)/shard_map/dot_general | solution.py:62
  18.2 2.8 %gather_fusion.1 = bf16[1280,64]{1,0:T(8,128)(2,1)S(1)} fusion(bf16[1024,64]{1,0:T(8,128)(2,1)S(1)} %fusion.1, s32[2048]{0:T(1024)S(1)} %pad_clamp_fusion), kind=kCustom, calls=%fused_computation.1 | custom fusion | bytes 332800 | tf_op jit(solution)/shard_map/gather | solution.py:66
  22.3 0.7 reduce.3
  23.0 0.8 reshape.186
  23.8 7.4 %all-to-all-start.1 = ((bf16[16,2,2560]{2,1,0:T(2,128)(2,1)}), bf16[16,2,2560]{2,1,0:T(2,128)(2,1)}, u32[]{:S(2)}, u32[]{:S(2)}) async-start(bf16[16,2,2560]{2,1,0:T(2,128)(2,1)} %reshape.186), calls=%async_computation.1 | async-start | bytes 327680 | tf_op jit(solution)/shard_map/all_to_all | solution.py:68
  31.2 4.2 %gather_fusion = bf16[1280,768]{1,0:T(8,128)(2,1)S(1)} fusion(bf16[1024,768]{1,0:T(8,128)(2,1)S(1)} %bitcast.28, s32[2048]{0:T(1024)S(1)} %pad_clamp_fusion), kind=kCustom, calls=%fused_computation | custom fusion | bytes 3937280 | tf_op jit(solution)/shard_map/gather | solution.py:61
  35.4 6.0 %all_to_all.17 = bf16[16,1,61440]{2,1,0:T(2,128)(2,1)} reshape(bf16[1280,768]{1,0:T(8,128)(2,1)S(1)} %gather_fusion) | data formatting | bytes 3932160 | tf_op jit(solution)/shard_map/all_to_all | solution.py:75
  41.5 12.6 %reduce.4 = bf16[16,61440]{1,0:T(8,128)(2,1)S(1)} reduce(bf16[16,1,61440]{2,1,0:T(2,128)(2,1)} %all_to_all.17, bf16[]{:T(256)} %broadcast.140), dimensions={1}, to_apply=%all_to_all.17.reduce_sub_computation | reduce | bytes 3932162 | tf_op jit(solution)/shard_map/all_to_all | solution.py:75
  54.1 2.6 %reshape.188 = bf16[16,2,30720]{2,1,0:T(2,128)(2,1)} reshape(bf16[16,61440]{1,0:T(8,128)(2,1)S(1)} %reduce.4) | data formatting | bytes 3932160
  56.7 6.0 %all-to-all-start = ((bf16[16,2,30720]{2,1,0:T(2,128)(2,1)}), bf16[16,2,30720]{2,1,0:T(2,128)(2,1)S(1)}, u32[]{:S(2)}, u32[]{:S(2)}) async-start(bf16[16,2,30720]{2,1,0:T(2,128)(2,1)} %reshape.188), calls=%async_computation | async-start | bytes 3932160 | tf_op jit(solution)/shard_map/all_to_all | solution.py:75
  62.7 2.1 %reshape.187 = bf16[16,1,5120]{2,1,0:T(2,128)(2,1)} reshape(bf16[16,2,2560]{2,1,0:T(2,128)(2,1)} %all-to-all-done.1) | data formatting | bytes 327680
  64.8 2.5 %reduce.2 = bf16[16,5120]{1,0:T(8,128)(2,1)} reduce(bf16[16,1,5120]{2,1,0:T(2,128)(2,1)} %reshape.187, bf16[]{:T(256)} %constant.51), dimensions={1}, to_apply=%all_to_all.15.reduce_sub_computation | reduce | bytes 327682 | tf_op jit(solution)/shard_map/all_to_all | solution.py:68
  67.3 1.9 %reshape.142 = bf16[16,80,64]{2,1,0:T(8,128)(2,1)} reshape(bf16[16,5120]{1,0:T(8,128)(2,1)} %reduce.2) | data formatting | bytes 327680 | tf_op jit(solution)/shard_map/reshape.4
  69.2 32.3 %all-to-all-done = bf16[16,2,30720]{2,1,0:T(2,128)(2,1)S(1)} async-done(((bf16[16,2,30720]{2,1,0:T(2,128)(2,1)}), bf16[16,2,30720]{2,1,0:T(2,128)(2,1)S(1)}, u32[]{:S(2)}, u32[]{:S(2)}) %all-to-all-start) | async-done | bytes 1966112 | tf_op jit(solution)/shard_map/all_to_all | solution.py:75
  101.5 6.6 %reshape.189 = bf16[16,1,61440]{2,1,0:T(2,128)(2,1)} reshape(bf16[16,2,30720]{2,1,0:T(2,128)(2,1)S(1)} %all-to-all-done) | data formatting | bytes 3932160
  108.1 12.0 %reduce.1 = bf16[16,61440]{1,0:T(8,128)(2,1)S(1)} reduce(bf16[16,1,61440]{2,1,0:T(2,128)(2,1)} %reshape.189, bf16[]{:T(256)} %constant.51), dimensions={1}, to_apply=%all_to_all.14.reduce_sub_computation | reduce | bytes 3932162 | tf_op jit(solution)/shard_map/all_to_all | solution.py:75
  120.0 1.9 %reshape.140 = bf16[1280,768]{1,0:T(8,128)(2,1)} reshape(bf16[16,61440]{1,0:T(8,128)(2,1)S(1)} %reduce.1) | data formatting | bytes 3932160 | tf_op jit(solution)/shard_map/reshape | solution.py:84
  122.0 2.3 %convolution_convert_fusion = bf16[1280,64]{0,1:T(8,128)(2,1)S(1)} fusion(bf16[1280,768]{1,0:T(8,128)(2,1)} %reshape.140, bf16[1,64,768]{2,1,0:T(8,128)(2,1)} %param.13), kind=kOutput, calls=%fused_computation.4 | convolution fusion | flops 125911040 | bytes 2228224 | tf_op jit(solution)/shard_map/dot_general | solution.py:83
  125.3 1.4 reduce.5
  126.7 18.4 %all_to_all.21 = bf16[16,2,2048]{2,1,0:T(2,128)(2,1)S(1)} all-to-all(bf16[16,2,2048]{2,1,0:T(2,128)(2,1)S(1)} %reshape.190), channel_id=1, replica_groups=mesh['groups'=2,'expert'=16,'dp'=1] {'expert'}, dimensions={0} | all-to-all | bytes 262144 | tf_op jit(solution)/shard_map/all_to_all | solution.py:90
  145.3 0.8 copy.53
  (32 shorter events, 5.3 us)
Async XLA Ops:
  0.0 31.2 %copy-start = (bf16[128,8,768]{2,1,0:T(8,128)(2,1)S(1)}, bf16[128,8,768]{2,1,0:T(8,128)(2,1)}, u32[]{:S(2)}) copy-start(bf16[128,8,768]{2,1,0:T(8,128)(2,1)} %param.8) | copy-start | bytes 4718596
  23.8 32.9 %all-to-all-start.1 = ((bf16[16,2,2560]{2,1,0:T(2,128)(2,1)}), bf16[16,2,2560]{2,1,0:T(2,128)(2,1)}, u32[]{:S(2)}, u32[]{:S(2)}) async-start(bf16[16,2,2560]{2,1,0:T(2,128)(2,1)} %reshape.186), calls=%async_computation.1 | async-start | bytes 327680 | tf_op jit(solution)/shard_map/all_to_all | solution.py:68
  56.7 44.8 %all-to-all-start = ((bf16[16,2,30720]{2,1,0:T(2,128)(2,1)}), bf16[16,2,30720]{2,1,0:T(2,128)(2,1)S(1)}, u32[]{:S(2)}, u32[]{:S(2)}) async-start(bf16[16,2,30720]{2,1,0:T(2,128)(2,1)} %reshape.188), calls=%async_computation | async-start | bytes 3932160 | tf_op jit(solution)/shard_map/all_to_all | solution.py:75
  122.0 2.7 %copy-start.1 = (bf16[16,80,64]{2,1,0:T(8,128)(2,1)S(1)}, bf16[16,80,64]{2,1,0:T(8,128)(2,1)}, u32[]{:S(2)}) copy-start(bf16[16,80,64]{2,1,0:T(8,128)(2,1)} %reshape.142) | copy-start | bytes 491524
where the time goes:
time: 147 us; the launch traced here: 146 us
  local copies, waits for them, and re-layouts  44.3 us (30%)
  other arithmetic  32.3 us (22%)
  waiting for transfers between devices  32.3 us (22%)
  blocking collectives  18.4 us (13%)
  starting transfers between devices  13.4 us (9%)
  matrix products  4.47 us (3%)
    all_to_all x1, waiting for transfers between devices, on_device(): lax.all_to_all(hidden_slots.reshape(expert_count, capacity * hidden_width...  32.3 us
    all_to_all x2, other arithmetic, on_device(): lax.all_to_all(hidden_slots.reshape(expert_count, capacity * hidden_width...  24.6 us
    all_to_all x1, blocking collectives, on_device(): lax.all_to_all(blocks.reshape(examples, expert_count, rank_dim * rank_dim...  18.4 us
    unnamed x10, local copies, waits for them, and re-layouts  12.3 us
    scatter x1, local copies, waits for them, and re-layouts, slot_layout(): filled = jnp.zeros((expert_count * capacity,), jnp.bfloat16).at[target].s...  7.59 us
    all_to_all x1, starting transfers between devices, on_device(): lax.all_to_all(scaled_slots.reshape(expert_count, capacity * examples * r...  7.4 us
    all_to_all x1, local copies, waits for them, and re-layouts, on_device(): lax.all_to_all(hidden_slots.reshape(expert_count, capacity * hidden_width...  6.03 us
    all_to_all x1, starting transfers between devices, on_device(): lax.all_to_all(hidden_slots.reshape(expert_count, capacity * hidden_width...  5.97 us
  transfers between devices with their start and end apart: 2, of which 1 were waited for; matrix products, arithmetic and copies ran while one was open for 18% of the time, Pallas kernels for 0%

commit v1 on v0

v1 whole, which is shorter than its diff:
```python
import functools

import jax
import jax.numpy as jnp
from jax import lax
from jax.experimental import pallas as pl
from jax.experimental.pallas import tpu as pltpu
from jax.sharding import PartitionSpec as P

ACROSS = (((1,), (1,)), ((), ()))


def route_columns(cot, basis_out, gates, ids, used):
    top, tokens = gates.shape
    routes = tokens * top
    rank = basis_out.shape[0]
    projected = lax.dot_general(cot, basis_out, ACROSS, preferred_element_type=jnp.float32)
    spread = (
        lax.broadcasted_iota(jnp.int32, (routes, tokens), 0) // top
        == lax.broadcasted_iota(jnp.int32, (routes, tokens), 1)
    ).astype(jnp.bfloat16)
    own = lax.broadcasted_iota(jnp.int32, (routes, top), 0) % top == lax.broadcasted_iota(
        jnp.int32, (routes, top), 1
    )

    def column(values):
        wide = lax.dot_general(spread, values, ACROSS, preferred_element_type=jnp.float32)
        return jnp.sum(jnp.where(own, wide, 0.0), axis=1, keepdims=True)

    gate = column(gates)
    expert = column(ids.astype(jnp.float32).astype(jnp.bfloat16))
    live = lax.broadcasted_iota(jnp.int32, (routes, 1), 0) // top < used
    weight = jnp.where(live, gate, 0.0)
    rows = jnp.broadcast_to(projected[:, None, :], (tokens, top, rank)).reshape(routes, rank)
    scaled = weight * rows
    return scaled.T.astype(jnp.bfloat16), jnp.broadcast_to(expert, (routes, 2 * rank))


def pair_sums(first, hidden, basis_pair, scaled_t, expert, acc_ref):
    rank = basis_pair.shape[0] // 2
    routes = hidden.shape[0]
    reduced = lax.dot_general(hidden, basis_pair, ACROSS, preferred_element_type=jnp.float32)
    lane = lax.broadcasted_iota(jnp.int32, (routes, 2 * rank), 1)
    names = (first + lane // rank).astype(jnp.float32)
    kept = jnp.where(expert == names, reduced, 0.0).astype(jnp.bfloat16)
    sums = jnp.dot(scaled_t, kept, preferred_element_type=jnp.float32)
    turned = pltpu.roll(sums, rank, 1)
    left = lax.broadcasted_iota(jnp.int32, (rank, 2 * rank), 1) < rank
    at = pl.multiple_of(first * rank, 2 * rank)
    acc_ref[pl.ds(at, rank), :] = jnp.where(left, sums, turned)
    acc_ref[pl.ds(at + rank, rank), :] = jnp.where(left, turned, sums)


def write_out(acc_ref, out_ref, rank):
    experts = out_ref.shape[1]
    left = lax.broadcasted_iota(jnp.int32, (experts, 2 * rank), 1) < rank
    for c in range(rank // 2):
        even = acc_ref[pl.ds(2 * c, experts, stride=rank), :]
        odd = acc_ref[pl.ds(2 * c + 1, experts, stride=rank), :]
        out_ref[0, :, pl.ds(c * 2 * rank, 2 * rank)] = jnp.where(left, even, odd).astype(out_ref.dtype)


def ring_kernel(
    parts,
    counts_ref, cot_ref, hidden_ref, gates_ref, ids_ref, out_basis_ref, in_basis_ref,
    out_ref,
    counts, cot, hidden, gates, ids, out_basis, basis, scaled_t, expert, acc,
    load_sem, z_send, z_recv, x_send, x_recv, c_send, c_recv,
):
    nz, nx, nc = parts
    rank, width = in_basis_ref.shape
    me = lax.axis_index("expert")
    z, x, c = me // (nx * nc), (me // nc) % nx, me % nc

    def place(pz, px, pc):
        return (pz * nx + px) * nc + pc

    def slot(e):
        return basis.at[pl.ds(pl.multiple_of(e * rank, rank), rank), :]

    loads = [
        pltpu.make_async_copy(src, dst, load_sem.at[i])
        for i, (src, dst) in enumerate(
            [
                (in_basis_ref, slot(me)),
                (cot_ref, cot),
                (out_basis_ref, out_basis),
                (gates_ref, gates),
                (ids_ref, ids),
                (counts_ref, counts),
                (hidden_ref, hidden),
            ]
        )
    ]
    for load in loads:
        load.start()

    x_peer, c_peer = place(z, 1 - x, c), place(z, x, 1 - c)
    peers = [place((z + s) % nz, x, c) for s in range(1, nz)] + [x_peer, c_peer]
    barrier = pltpu.get_barrier_semaphore()
    for peer in peers:
        pl.semaphore_signal(
            barrier, inc=1, device_id={"expert": peer}, device_id_type=pl.DeviceIdType.MESH
        )
    pl.semaphore_wait(barrier, len(peers))

    def send(source, e, peer, send_sem, recv_sem):
        copy = pltpu.make_async_remote_copy(
            src_ref=source,
            dst_ref=slot(e),
            send_sem=send_sem,
            recv_sem=recv_sem,
            device_id={"expert": peer},
            device_id_type=pl.DeviceIdType.MESH,
        )
        copy.start()
        return copy

    column = [place((z - s + nz) % nz, x, c) for s in range(nz)]
    across = [place((z - s + nz) % nz, 1 - x, c) for s in range(nz)]
    z_copy, x_copy, c_copy = {}, {}, {}
    order = [1, 3, 2] if nz == 4 else list(range(1, nz))
    for s in order:
        z_copy[s] = send(in_basis_ref, me, place((z + s) % nz, x, c), z_send.at[s - 1], z_recv.at[s - 1])
    x_copy[0] = send(in_basis_ref, me, x_peer, x_send.at[0], x_recv.at[0])
    c_copy[0] = send(in_basis_ref, me, c_peer, c_send.at[0], c_recv.at[0])

    for load in loads[1:6]:
        load.wait()
    scaled_t[...], expert[...] = route_columns(
        cot[...], out_basis[...], gates[...], ids[...], counts[0]
    )
    loads[6].wait()
    loads[0].wait()

    def pair(e):
        first = e // 2 * 2
        pair_sums(
            first,
            hidden[...],
            basis[pl.ds(pl.multiple_of(first * rank, 2 * rank), 2 * rank), :],
            scaled_t[...],
            expert[...],
            acc,
        )

    for s in order:
        z_copy[s].wait_recv()
        x_copy[s] = send(slot(column[s]), column[s], x_peer, x_send.at[s], x_recv.at[s])
        c_copy[s] = send(slot(column[s]), column[s], c_peer, c_send.at[s], c_recv.at[s])
    for s in [0] + order:
        x_copy[s].wait_recv()
        c_copy[nz + s] = send(
            slot(across[s]), across[s], c_peer, c_send.at[nz + s], c_recv.at[nz + s]
        )
        c_copy[s].wait_recv()
        pair(column[s])
    for s in [0] + order:
        c_copy[nz + s].wait_recv()
        pair(across[s])
    write_out(acc, out_ref, rank)
    for copies in (z_copy, x_copy, c_copy):
        for copy in copies.values():
            copy.wait_send()


def local_kernel(
    counts_ref, cot, hidden, gates, ids, out_basis, basis, out_ref, scaled_t, expert, acc
):
    rank = out_basis.shape[0]
    experts = out_ref.shape[1]
    scaled_t[...], expert[...] = route_columns(
        cot[...], out_basis[...], gates[...], ids[...], counts_ref[0]
    )

    @pl.loop(0, experts // 2)
    def _(j):
        pair_sums(
            2 * j,
            hidden[...],
            basis[pl.ds(pl.multiple_of(2 * j * rank, 2 * rank), 2 * rank), :],
            scaled_t[...],
            expert[...],
            acc,
        )

    write_out(acc, out_ref, rank)


def on_device(cotangent, hidden, gates, expert_ids, counts, proj_out, proj_in):
    tokens, top = expert_ids.shape
    routes = tokens * top
    model = cotangent.shape[1]
    rank = proj_out.shape[0]
    width = hidden.shape[2]
    experts = lax.axis_size("expert")
    dp = lax.axis_size("dp")
    bf16 = jnp.bfloat16
    if dp > 1:
        proj_out = lax.all_gather(proj_out, "dp", axis=1, tiled=True)
        proj_in = lax.all_gather(proj_in, "dp", axis=2, tiled=True)
    hidden = hidden.reshape(routes, width)
    gates, expert_ids = gates.T, expert_ids.T
    out_shape = jax.ShapeDtypeStruct((1, experts, rank * rank), bf16)
    tail = [
        pltpu.VMEM((rank, routes), bf16),
        pltpu.VMEM((routes, 2 * rank), jnp.float32),
        pltpu.VMEM((experts * rank, 2 * rank), jnp.float32),
    ]
    cost = pl.CostEstimate(
        flops=2 * routes * experts * rank * (width + rank),
        bytes_accessed=2 * (tokens * model + routes * width + experts * rank * width),
        transcendentals=0,
    )
    smem = pl.BlockSpec(memory_space=pltpu.SMEM)
    vmem = pl.BlockSpec(memory_space=pltpu.VMEM)
    anywhere = pl.BlockSpec(memory_space=pl.ANY)
    if experts != 16 or dp > 1:
        basis = lax.all_gather(proj_in.reshape(rank, width), "expert", axis=0, tiled=True)
        return pl.pallas_call(
            local_kernel,
            out_shape=out_shape,
            in_specs=[smem] + [vmem] * 6,
            out_specs=vmem,
            scratch_shapes=tail,
            cost_estimate=cost,
            compiler_params=pltpu.CompilerParams(vmem_limit_bytes=48 << 20),
        )(counts, cotangent, hidden, gates, expert_ids, proj_out, basis)
    parts = (experts // 4, 2, 2)
    dma = pltpu.SemaphoreType.DMA
    nz = parts[0]
    return pl.pallas_call(
        functools.partial(ring_kernel, parts),
        out_shape=out_shape,
        in_specs=[anywhere] * 7,
        out_specs=vmem,
        scratch_shapes=[
            pltpu.SMEM((1,), jnp.int32),
            pltpu.VMEM((tokens, model), bf16),
            pltpu.VMEM((routes, width), bf16),
            pltpu.VMEM((top, tokens), bf16),
            pltpu.VMEM((top, tokens), jnp.int32),
            pltpu.VMEM((rank, model), bf16),
            pltpu.VMEM((experts * rank, width), bf16),
        ]
        + tail
        + [
            dma((7,)),
            dma((nz - 1,)),
            dma((nz - 1,)),
            dma((nz,)),
            dma((nz,)),
            dma((2 * nz,)),
            dma((2 * nz,)),
        ],
        cost_estimate=cost,
        compiler_params=pltpu.CompilerParams(
            collective_id=0, has_side_effects=True, vmem_limit_bytes=40 << 20
        ),
    )(counts, cotangent, hidden, gates, expert_ids, proj_out, proj_in.reshape(rank, width))


def solution(mesh):
    rows = ("groups", "expert", "dp")
    placed = (
        P(rows, None),
        P(rows, None, None),
        P(rows, None),
        P(rows, None),
        P(rows),
        P(None, "dp"),
        P("expert", None, "dp"),
    )
    return jax.shard_map(
        on_device,
        mesh=mesh,
        in_specs=placed,
        out_specs=P(rows, None, None),
        check_vma=False,
    )
```

time: 147 us -> 32.9 us (0.22)
  local copies, waits for them, and re-layouts: 44.3 us -> 6.58 us
  other arithmetic: 32.3 us -> 0 us
  waiting for transfers between devices: 32.3 us -> 0 us
  Pallas kernels: 0 us -> 25.3 us
  blocking collectives: 18.4 us -> 0 us
  starting transfers between devices: 13.4 us -> 0 us
  matrix products: 4.47 us -> 0 us
    all_to_all x2 -> x0, waiting for transfers between devices: 32.3 us -> none  [the longest x1 32.3 us: on_device(): lax.all_to_all(hidden_slots.reshape(expert_count, capacity * hidden_width...]
    all_to_all x3 -> x0, other arithmetic: 27.1 us -> none  [the longest x2 24.6 us: on_device(): lax.all_to_all(hidden_slots.reshape(expert_count, capacity * hidden_width...]
    pallas_call x0 -> x1, Pallas kernels: none -> 25.3 us  [on_device(): pl.pallas_call(functools.partial(ring_kernel, parts), out_shape=out_shape...]
    all_to_all x1 -> x0, blocking collectives: 18.4 us -> none  [on_device(): lax.all_to_all(blocks.reshape(examples, expert_count, rank_dim * rank_dim...]
    all_to_all x2 -> x0, starting transfers between devices: 13.4 us -> none  [the longest x1 7.4 us: on_device(): lax.all_to_all(scaled_slots.reshape(expert_count, capacity * examples * r...]
    scatter x2 -> x0, local copies, waits for them, and re-layouts: 11.9 us -> none  [the longest x1 7.59 us: slot_layout(): filled = jnp.zeros((expert_count * capacity,), jnp.bfloat16).at[target].s...]
    gather x3 -> x0, local copies, waits for them, and re-layouts: 7.27 us -> none  [the longest x1 4.24 us: on_device(): hidden_slots = hidden.reshape(routes, hidden_width)[route_of]]
    all_to_all x2 -> x0, local copies, waits for them, and re-layouts: 6.84 us -> none  [the longest x1 6.03 us: on_device(): lax.all_to_all(hidden_slots.reshape(expert_count, capacity * hidden_width...]
  transfers between devices with their start and end apart: 2 -> 0, of which waited for: 1 -> 0; matrix products, arithmetic and copies ran while one was open for 18% -> 0% of each run, Pallas kernels for 0% -> 0%
where the time goes in v1:
time: 32.9 us; the launch traced here: 32.6 us
  Pallas kernels  25.3 us (77%)
  local copies, waits for them, and re-layouts  6.58 us (20%)
  between operations  0.67 us (2%)
    pallas_call x1, Pallas kernels, on_device(): pl.pallas_call(functools.partial(ring_kernel, parts), out_shape=out_shape...  25.3 us
    unnamed x13, local copies, waits for them, and re-layouts  6.58 us

profile of v1, /device:TPU:0, one launch (start us, length us, event | category | flops | bytes accessed | tf_op | source)
XLA Modules:
  0.0 32.6 jit_solution(1322173069697073890)
XLA Ops:
  0.7 0.0 copy-start
  0.7 1.4 %copy-done = bf16[128,8,768]{2,1,0:T(8,128)(2,1)S(1)} copy-done((bf16[128,8,768]{2,1,0:T(8,128)(2,1)S(1)}, bf16[128,8,768]{2,1,0:T(8,128)(2,1)}, u32[]{:S(2)}) %copy-start) | copy-done | bytes 1572888
  2.1 0.0 copy-start.1
  2.1 1.2 %copy-done.1 = bf16[128,4096]{1,0:T(8,128)(2,1)S(1)} copy-done((bf16[128,4096]{1,0:T(8,128)(2,1)S(1)}, bf16[128,4096]{1,0:T(8,128)(2,1)}, u32[]{:S(2)}) %copy-start.1) | copy-done | bytes 1048600
  3.3 0.0 copy-start.2
  3.3 1.0 %copy-done.2 = bf16[64,4096]{1,0:T(8,128)(2,1)S(1)} copy-done((bf16[64,4096]{1,0:T(8,128)(2,1)S(1)}, bf16[64,4096]{1,0:T(8,128)(2,1)}, u32[]{:S(2)}) %copy-start.2) | copy-done | bytes 524312
  4.3 0.0 copy-start.3
  4.3 0.9 %copy-done.3 = bf16[1,64,768]{2,1,0:T(8,128)(2,1)S(1)} copy-done((bf16[1,64,768]{2,1,0:T(8,128)(2,1)S(1)}, bf16[1,64,768]{2,1,0:T(8,128)(2,1)}, u32[]{:S(2)}) %copy-start.3) | copy-done | bytes 98328
  5.2 0.0 copy-start.4
  5.2 0.7 %copy-done.4 = s32[128,8]{0,1:T(8,128)S(1)} copy-done((s32[128,8]{0,1:T(8,128)S(1)}, s32[128,8]{0,1:T(8,128)}, u32[]{:S(2)}) %copy-start.4) | copy-done | bytes 4120
  5.9 0.0 copy-start.5
  5.9 0.7 %copy-done.5 = bf16[128,8]{0,1:T(8,128)(2,1)S(1)} copy-done((bf16[128,8]{0,1:T(8,128)(2,1)S(1)}, bf16[128,8]{0,1:T(8,128)(2,1)}, u32[]{:S(2)}) %copy-start.5) | copy-done | bytes 2072
  6.6 25.3 %shard_map.73 = bf16[1,16,4096]{2,1,0:T(8,128)(2,1)S(1)} custom-call(s32[1]{0:T(128)S(6)} %copy.9.counts_ref, bf16[128,4096]{1,0:T(8,128)(2,1)S(1)} %copy-done.1, bf16[1024,768]{1,0:T(8,128)(2,1)S(1)} %bitcast.4, bf16[8,128]{1,0:T(8,128)(2,1)S(1)} %bitcast.7, s32[8,128]{1,0:T(8,128)S(1)} %bitcast.6, bf16[64,4096]{1,0:T(8,128)(2,1)S(1)} %copy-done.2, ...), custom_call_target="tpu_custom_call" | custom-call | flops 1744830464 | bytes 4194304 | tf_op jit(solution)/shard_map/pallas_call | solution.py:232
  31.9 0.7 %copy.10 = bf16[1,16,4096]{2,1,0:T(8,128)(2,1)} copy(bf16[1,16,4096]{2,1,0:T(8,128)(2,1)S(1)} %shard_map.73) | data formatting | bytes 262144
Async XLA Ops:
  0.7 1.4 %copy-start = (bf16[128,8,768]{2,1,0:T(8,128)(2,1)S(1)}, bf16[128,8,768]{2,1,0:T(8,128)(2,1)}, u32[]{:S(2)}) copy-start(bf16[128,8,768]{2,1,0:T(8,128)(2,1)} %param.8) | copy-start | bytes 4718596
  2.1 1.2 %copy-start.1 = (bf16[128,4096]{1,0:T(8,128)(2,1)S(1)}, bf16[128,4096]{1,0:T(8,128)(2,1)}, u32[]{:S(2)}) copy-start(bf16[128,4096]{1,0:T(8,128)(2,1)} %cot_ref.1) | copy-start | bytes 3145732
  3.3 1.0 %copy-start.2 = (bf16[64,4096]{1,0:T(8,128)(2,1)S(1)}, bf16[64,4096]{1,0:T(8,128)(2,1)}, u32[]{:S(2)}) copy-start(bf16[64,4096]{1,0:T(8,128)(2,1)} %out_basis_ref.1) | copy-start | bytes 1572868
  4.3 0.9 %copy-start.3 = (bf16[1,64,768]{2,1,0:T(8,128)(2,1)S(1)}, bf16[1,64,768]{2,1,0:T(8,128)(2,1)}, u32[]{:S(2)}) copy-start(bf16[1,64,768]{2,1,0:T(8,128)(2,1)} %param.13) | copy-start | bytes 294916
  5.2 0.7 %copy-start.4 = (s32[128,8]{0,1:T(8,128)S(1)}, s32[128,8]{0,1:T(8,128)}, u32[]{:S(2)}) copy-start(s32[128,8]{0,1:T(8,128)} %param.10) | copy-start | bytes 12292
  5.9 0.7 %copy-start.5 = (bf16[128,8]{0,1:T(8,128)(2,1)S(1)}, bf16[128,8]{0,1:T(8,128)(2,1)}, u32[]{:S(2)}) copy-start(bf16[128,8]{0,1:T(8,128)(2,1)} %param.9) | copy-start | bytes 6148

commit v2 on v1

--- a/solution.py
+++ b/solution.py
@@ -36,19 +36,25 @@
     return scaled.T.astype(jnp.bfloat16), jnp.broadcast_to(expert, (routes, 2 * rank))
 
 
-def pair_sums(first, hidden, basis_pair, scaled_t, expert, acc_ref):
-    rank = basis_pair.shape[0] // 2
+def group_sums(first, hidden, basis, scaled_t, expert, acc_ref):
+    rank = scaled_t.shape[0]
     routes = hidden.shape[0]
-    reduced = lax.dot_general(hidden, basis_pair, ACROSS, preferred_element_type=jnp.float32)
-    lane = lax.broadcasted_iota(jnp.int32, (routes, 2 * rank), 1)
-    names = (first + lane // rank).astype(jnp.float32)
-    kept = jnp.where(expert == names, reduced, 0.0).astype(jnp.bfloat16)
+    pair = 2 * rank
+    reduced = lax.dot_general(hidden, basis, ACROSS, preferred_element_type=jnp.float32)
+    lane = lax.broadcasted_iota(jnp.int32, (routes, pair), 1)
+    left = lax.broadcasted_iota(jnp.int32, (rank, pair), 1) < rank
+    kept = []
+    for p in range(basis.shape[0] // pair):
+        names = (first + 2 * p + lane // rank).astype(jnp.float32)
+        kept.append(jnp.where(expert == names, reduced[:, p * pair : (p + 1) * pair], 0.0))
+    kept = jnp.concatenate(kept, axis=1).astype(jnp.bfloat16)
     sums = jnp.dot(scaled_t, kept, preferred_element_type=jnp.float32)
-    turned = pltpu.roll(sums, rank, 1)
-    left = lax.broadcasted_iota(jnp.int32, (rank, 2 * rank), 1) < rank
-    at = pl.multiple_of(first * rank, 2 * rank)
-    acc_ref[pl.ds(at, rank), :] = jnp.where(left, sums, turned)
-    acc_ref[pl.ds(at + rank, rank), :] = jnp.where(left, turned, sums)
+    for p in range(basis.shape[0] // pair):
+        part = sums[:, p * pair : (p + 1) * pair]
+        turned = pltpu.roll(part, rank, 1)
+        at = pl.multiple_of((first + 2 * p) * rank, pair)
+        acc_ref[pl.ds(at, rank), :] = jnp.where(left, part, turned)
+        acc_ref[pl.ds(at + rank, rank), :] = jnp.where(left, turned, part)
 
 
 def write_out(acc_ref, out_ref, rank):
@@ -65,24 +71,29 @@
     counts_ref, cot_ref, hidden_ref, gates_ref, ids_ref, out_basis_ref, in_basis_ref,
     out_ref,
     counts, cot, hidden, gates, ids, out_basis, basis, scaled_t, expert, acc,
-    load_sem, z_send, z_recv, x_send, x_recv, c_send, c_recv,
+    load_sem, z_send, z_recv, x_send, x_recv, y_send, y_recv, c_send, c_recv,
 ):
     nz, nx, nc = parts
     rank, width = in_basis_ref.shape
+    half = rank // 2
     me = lax.axis_index("expert")
+    y = lax.axis_index("groups")
     z, x, c = me // (nx * nc), (me // nc) % nx, me % nc
 
     def place(pz, px, pc):
         return (pz * nx + px) * nc + pc
 
-    def slot(e):
+    def whole(e):
         return basis.at[pl.ds(pl.multiple_of(e * rank, rank), rank), :]
+
+    def piece(e, h):
+        return basis.at[pl.ds(pl.multiple_of(e * rank + h * half, half), half), :]
 
     loads = [
         pltpu.make_async_copy(src, dst, load_sem.at[i])
         for i, (src, dst) in enumerate(
             [
-                (in_basis_ref, slot(me)),
+                (in_basis_ref, whole(me)),
                 (cot_ref, cot),
                 (out_basis_ref, out_basis),
                 (gates_ref, gates),
@@ -95,35 +106,48 @@
     for load in loads:
         load.start()
 
-    x_peer, c_peer = place(z, 1 - x, c), place(z, x, 1 - c)
-    peers = [place((z + s) % nz, x, c) for s in range(1, nz)] + [x_peer, c_peer]
+    x_peer = {"expert": place(z, 1 - x, c)}
+    c_peer = {"expert": place(z, x, 1 - c)}
+    y_peer = {"groups": 1 - y}
+    z_peer = {s: {"expert": place((z + s) % nz, x, c)} for s in range(1, nz)}
+    peers = list(z_peer.values()) + [x_peer, y_peer, c_peer]
     barrier = pltpu.get_barrier_semaphore()
     for peer in peers:
-        pl.semaphore_signal(
-            barrier, inc=1, device_id={"expert": peer}, device_id_type=pl.DeviceIdType.MESH
-        )
+        pl.semaphore_signal(barrier, inc=1, device_id=peer, device_id_type=pl.DeviceIdType.MESH)
     pl.semaphore_wait(barrier, len(peers))
 
-    def send(source, e, peer, send_sem, recv_sem):
+    started = []
+
+    def send(source, target, peer, sems, i):
         copy = pltpu.make_async_remote_copy(
             src_ref=source,
-            dst_ref=slot(e),
-            send_sem=send_sem,
-            recv_sem=recv_sem,
-            device_id={"expert": peer},
+            dst_ref=target,
+            send_sem=sems[0].at[i],
+            recv_sem=sems[1].at[i],
+            device_id=peer,
             device_id_type=pl.DeviceIdType.MESH,
         )
         copy.start()
+        started.append(copy)
         return copy
 
+    zs, xs, ys, cs = (z_send, z_recv), (x_send, x_recv), (y_send, y_recv), (c_send, c_recv)
     column = [place((z - s + nz) % nz, x, c) for s in range(nz)]
     across = [place((z - s + nz) % nz, 1 - x, c) for s in range(nz)]
-    z_copy, x_copy, c_copy = {}, {}, {}
     order = [1, 3, 2] if nz == 4 else list(range(1, nz))
-    for s in order:
-        z_copy[s] = send(in_basis_ref, me, place((z + s) % nz, x, c), z_send.at[s - 1], z_recv.at[s - 1])
-    x_copy[0] = send(in_basis_ref, me, x_peer, x_send.at[0], x_recv.at[0])
-    c_copy[0] = send(in_basis_ref, me, c_peer, c_send.at[0], c_recv.at[0])
+    z_copy, x_copy, y_copy, c_copy = {}, {}, {}, {}
+
+    def to_y(i, e):
+        y_copy[i] = send(piece(e, y), piece(e, y), y_peer, ys, i)
+
+    def to_c(i, e, h):
+        c_copy[i] = send(piece(e, h), piece(e, h), c_peer, cs, i)
+
+    mine = in_basis_ref.at[pl.ds(pl.multiple_of(y * half, half), half), :]
+    for s in order:
+        z_copy[s] = send(mine, piece(me, y), z_peer[s], zs, s - 1)
+    x_copy[0] = send(in_basis_ref, whole(me), x_peer, xs, 0)
+    c_copy[0] = send(in_basis_ref, whole(me), c_peer, cs, 0)
 
     for load in loads[1:6]:
         load.wait()
@@ -133,35 +157,53 @@
     loads[6].wait()
     loads[0].wait()
 
-    def pair(e):
-        first = e // 2 * 2
-        pair_sums(
+    def quad(s):
+        first = (z - s + nz) % nz * (nx * nc)
+        rows = nx * nc * rank
+        group_sums(
             first,
             hidden[...],
-            basis[pl.ds(pl.multiple_of(first * rank, 2 * rank), 2 * rank), :],
+            basis[pl.ds(pl.multiple_of(first * rank, rows), rows), :],
             scaled_t[...],
             expert[...],
             acc,
         )
 
-    for s in order:
+    def from_z(s):
         z_copy[s].wait_recv()
-        x_copy[s] = send(slot(column[s]), column[s], x_peer, x_send.at[s], x_recv.at[s])
-        c_copy[s] = send(slot(column[s]), column[s], c_peer, c_send.at[s], c_recv.at[s])
-    for s in [0] + order:
+        x_copy[s] = send(piece(column[s], y), piece(column[s], y), x_peer, xs, s)
+        to_y(s - 1, column[s])
+        to_c(4 * s, column[s], y)
+
+    def from_x(s):
         x_copy[s].wait_recv()
-        c_copy[nz + s] = send(
-            slot(across[s]), across[s], c_peer, c_send.at[nz + s], c_recv.at[nz + s]
-        )
-        c_copy[s].wait_recv()
-        pair(column[s])
-    for s in [0] + order:
-        c_copy[nz + s].wait_recv()
-        pair(across[s])
+        to_y(nz + s - 2, across[s])
+        to_c(4 * s + 1, across[s], y)
+
+    for s in order[:-1]:
+        from_z(s)
+    x_copy[0].wait_recv()
+    c_copy[1] = send(whole(across[0]), whole(across[0]), c_peer, cs, 1)
+    for s in order[-1:]:
+        from_z(s)
+    c_copy[0].wait_recv()
+    c_copy[1].wait_recv()
+    quad(0)
+    for s in order:
+        from_x(s)
+    for s in order:
+        y_copy[s - 1].wait_recv()
+        to_c(4 * s + 2, column[s], 1 - y)
+    for s in order:
+        y_copy[nz + s - 2].wait_recv()
+        to_c(4 * s + 3, across[s], 1 - y)
+    for s in order:
+        for i in range(4):
+            c_copy[4 * s + i].wait_recv()
+        quad(s)
     write_out(acc, out_ref, rank)
-    for copies in (z_copy, x_copy, c_copy):
-        for copy in copies.values():
-            copy.wait_send()
+    for copy in started:
+        copy.wait_send()
 
 
 def local_kernel(
@@ -173,12 +215,12 @@
         cot[...], out_basis[...], gates[...], ids[...], counts_ref[0]
     )
 
-    @pl.loop(0, experts // 2)
+    @pl.loop(0, experts // 4)
     def _(j):
-        pair_sums(
-            2 * j,
+        group_sums(
+            4 * j,
             hidden[...],
-            basis[pl.ds(pl.multiple_of(2 * j * rank, 2 * rank), 2 * rank), :],
+            basis[pl.ds(pl.multiple_of(4 * j * rank, 4 * rank), 4 * rank), :],
             scaled_t[...],
             expert[...],
             acc,
@@ -215,7 +257,7 @@
     smem = pl.BlockSpec(memory_space=pltpu.SMEM)
     vmem = pl.BlockSpec(memory_space=pltpu.VMEM)
     anywhere = pl.BlockSpec(memory_space=pl.ANY)
-    if experts != 16 or dp > 1:
+    if experts != 16 or dp > 1 or lax.axis_size("groups") != 2:
         basis = lax.all_gather(proj_in.reshape(rank, width), "expert", axis=0, tiled=True)
         return pl.pallas_call(
             local_kernel,
@@ -250,12 +292,14 @@
             dma((nz - 1,)),
             dma((nz,)),
             dma((nz,)),
-            dma((2 * nz,)),
-            dma((2 * nz,)),
+            dma((2 * nz - 2,)),
+            dma((2 * nz - 2,)),
+            dma((4 * nz,)),
+            dma((4 * nz,)),
         ],
         cost_estimate=cost,
         compiler_params=pltpu.CompilerParams(
-            collective_id=0, has_side_effects=True, vmem_limit_bytes=40 << 20
+            collective_id=0, has_side_effects=True, vmem_limit_bytes=63 << 20
         ),
     )(counts, cotangent, hidden, gates, expert_ids, proj_out, proj_in.reshape(rank, width))
 

time: 32.9 us -> 25.1 us (0.76)
  local copies, waits for them, and re-layouts: 6.58 us -> 1.57 us
  Pallas kernels: 25.3 us -> 22.7 us
    unnamed x13 -> x1, local copies, waits for them, and re-layouts: 6.58 us -> 1.57 us
    pallas_call x1, Pallas kernels: 25.3 us -> 22.7 us  [on_device(): pl.pallas_call(functools.partial(ring_kernel, parts), out_shape=out_shape...]
where the time goes in v2:
time: 25.1 us; the launch traced here: 24.9 us
  Pallas kernels  22.7 us (90%)
  local copies, waits for them, and re-layouts  1.57 us (6%)
  between operations  0.66 us (3%)
    pallas_call x1, Pallas kernels, on_device(): pl.pallas_call(functools.partial(ring_kernel, parts), out_shape=out_shape...  22.7 us
    unnamed x1, local copies, waits for them, and re-layouts  1.57 us

profile of v2, /device:TPU:0, one launch (start us, length us, event | category | flops | bytes accessed | tf_op | source)
XLA Modules:
  0.0 24.9 jit_solution(17594465940061992246)
XLA Ops:
  0.7 22.7 %shard_map.73 = bf16[1,16,4096]{2,1,0:T(8,128)(2,1)} custom-call(s32[1]{0:T(128)S(6)} %copy.9.counts_ref, bf16[128,4096]{1,0:T(8,128)(2,1)} %cot_ref.1, bf16[1024,768]{1,0:T(8,128)(2,1)} %bitcast.4, bf16[8,128]{1,0:T(8,128)(2,1)} %bitcast.7, s32[8,128]{1,0:T(8,128)} %bitcast.6, bf16[64,4096]{1,0:T(8,128)(2,1)} %out_basis_ref.1, bf16[64,768]{1,0:T(8,128)(2,1)} %bitcast.5), custom_call_target="tpu_custom_call" | custom-call | flops 1744830464 | bytes 4194304 | tf_op jit(solution)/shard_map/pallas_call | solution.py:274
  23.4 1.6 %copy.10 = bf16[1,16,4096]{2,1,0:T(8,128)(2,1)} copy(bf16[1,16,4096]{2,1,0:T(8,128)(2,1)} %shard_map.73) | data formatting | bytes 262144

commit v3 on v2

--- a/solution.py
+++ b/solution.py
@@ -109,8 +109,10 @@
     x_peer = {"expert": place(z, 1 - x, c)}
     c_peer = {"expert": place(z, x, 1 - c)}
     y_peer = {"groups": 1 - y}
-    z_peer = {s: {"expert": place((z + s) % nz, x, c)} for s in range(1, nz)}
-    peers = list(z_peer.values()) + [x_peer, y_peer, c_peer]
+    d_peer = {"groups": 1 - y, "expert": place(z, 1 - x, c)}
+    along = [z, z + 1 - 2 * (z % 2), (z + 2) % nz, nz - 1 - z]
+    z_peer = {s: {"expert": place(along[s], x, c)} for s in range(1, nz)}
+    peers = list(z_peer.values()) + [x_peer, y_peer, c_peer, d_peer]
     barrier = pltpu.get_barrier_semaphore()
     for peer in peers:
         pl.semaphore_signal(barrier, inc=1, device_id=peer, device_id_type=pl.DeviceIdType.MESH)
@@ -132,13 +134,13 @@
         return copy
 
     zs, xs, ys, cs = (z_send, z_recv), (x_send, x_recv), (y_send, y_recv), (c_send, c_recv)
-    column = [place((z - s + nz) % nz, x, c) for s in range(nz)]
-    across = [place((z - s + nz) % nz, 1 - x, c) for s in range(nz)]
-    order = [1, 3, 2] if nz == 4 else list(range(1, nz))
+    column = [place(along[s], x, c) for s in range(nz)]
+    across = [place(along[s], 1 - x, c) for s in range(nz)]
+    order, diagonal = [1, 2, 3], []
     z_copy, x_copy, y_copy, c_copy = {}, {}, {}, {}
 
-    def to_y(i, e):
-        y_copy[i] = send(piece(e, y), piece(e, y), y_peer, ys, i)
+    def to_y(i, e, peer):
+        y_copy[i] = send(piece(e, y), piece(e, y), peer, ys, i)
 
     def to_c(i, e, h):
         c_copy[i] = send(piece(e, h), piece(e, h), c_peer, cs, i)
@@ -158,7 +160,7 @@
     loads[0].wait()
 
     def quad(s):
-        first = (z - s + nz) % nz * (nx * nc)
+        first = along[s] * (nx * nc)
         rows = nx * nc * rank
         group_sums(
             first,
@@ -172,35 +174,47 @@
     def from_z(s):
         z_copy[s].wait_recv()
         x_copy[s] = send(piece(column[s], y), piece(column[s], y), x_peer, xs, s)
-        to_y(s - 1, column[s])
+        to_y(s - 1, column[s], y_peer)
+        if s in diagonal:
+            to_y(nz + s - 2, column[s], d_peer)
         to_c(4 * s, column[s], y)
 
     def from_x(s):
         x_copy[s].wait_recv()
-        to_y(nz + s - 2, across[s])
+        if s not in diagonal:
+            to_y(nz + s - 2, across[s], y_peer)
         to_c(4 * s + 1, across[s], y)
+
+    def from_y(s):
+        y_copy[s - 1].wait_recv()
+        to_c(4 * s + 2, column[s], 1 - y)
+
+    def from_far(s):
+        y_copy[nz + s - 2].wait_recv()
+        to_c(4 * s + 3, across[s], 1 - y)
+
+    def finish(s):
+        for i in range(4):
+            c_copy[4 * s + i].wait_recv()
+        quad(s)
 
     for s in order[:-1]:
         from_z(s)
     x_copy[0].wait_recv()
     c_copy[1] = send(whole(across[0]), whole(across[0]), c_peer, cs, 1)
-    for s in order[-1:]:
-        from_z(s)
+    from_z(order[-1])
     c_copy[0].wait_recv()
     c_copy[1].wait_recv()
     quad(0)
     for s in order:
         from_x(s)
-    for s in order:
-        y_copy[s - 1].wait_recv()
-        to_c(4 * s + 2, column[s], 1 - y)
-    for s in order:
-        y_copy[nz + s - 2].wait_recv()
-        to_c(4 * s + 3, across[s], 1 - y)
-    for s in order:
-        for i in range(4):
-            c_copy[4 * s + i].wait_recv()
-        quad(s)
+        from_y(s)
+    for s in order[:-1]:
+        from_far(s)
+    finish(order[0])
+    from_far(order[-1])
+    for s in order[1:]:
+        finish(s)
     write_out(acc, out_ref, rank)
     for copy in started:
         copy.wait_send()
@@ -243,7 +257,7 @@
         proj_in = lax.all_gather(proj_in, "dp", axis=2, tiled=True)
     hidden = hidden.reshape(routes, width)
     gates, expert_ids = gates.T, expert_ids.T
-    out_shape = jax.ShapeDtypeStruct((1, experts, rank * rank), bf16)
+    out_shape = pltpu.VMEM((1, experts, rank * rank), bf16)
     tail = [
         pltpu.VMEM((rank, routes), bf16),
         pltpu.VMEM((routes, 2 * rank), jnp.float32),

time: 25.1 us -> 23 us (0.916)
  Pallas kernels: 22.7 us -> 21.5 us
  local copies, waits for them, and re-layouts: 1.57 us -> 0.66 us
    pallas_call x1, Pallas kernels: 22.7 us -> 21.5 us  [on_device(): pl.pallas_call(functools.partial(ring_kernel, parts), out_shape=out_shape...]
    unnamed x1, local copies, waits for them, and re-layouts: 1.57 us -> 0.66 us
where the time goes in v3:
time: 23 us; the launch traced here: 22.9 us
  Pallas kernels  21.5 us (93%)
  local copies, waits for them, and re-layouts  0.66 us (3%)
  between operations  0.66 us (3%)
    pallas_call x1, Pallas kernels, on_device(): pl.pallas_call(functools.partial(ring_kernel, parts), out_shape=out_shape...  21.5 us
    unnamed x1, local copies, waits for them, and re-layouts  0.66 us

profile of v3, /device:TPU:0, one launch (start us, length us, event | category | flops | bytes accessed | tf_op | source)
XLA Modules:
  0.0 22.9 jit_solution(5535757134165415781)
XLA Ops:
  0.7 21.5 %shard_map.73 = bf16[1,16,4096]{2,1,0:T(8,128)(2,1)S(1)} custom-call(s32[1]{0:T(128)S(6)} %copy.10.counts_ref, bf16[128,4096]{1,0:T(8,128)(2,1)} %cot_ref.1, bf16[1024,768]{1,0:T(8,128)(2,1)} %bitcast.4, bf16[8,128]{1,0:T(8,128)(2,1)} %bitcast.7, s32[8,128]{1,0:T(8,128)} %bitcast.6, bf16[64,4096]{1,0:T(8,128)(2,1)} %out_basis_ref.1, bf16[64,768]{1,0:T(8,128)(2,1)} %bitcast.5), custom_call_target="tpu_custom_call" | custom-call | flops 1744830464 | bytes 4194304 | tf_op jit(solution)/shard_map/pallas_call | solution.py:288
  22.2 0.7 %copy.9 = bf16[1,16,4096]{2,1,0:T(8,128)(2,1)} copy(bf16[1,16,4096]{2,1,0:T(8,128)(2,1)S(1)} %shard_map.73) | data formatting | bytes 262144

commit v4 on v3

--- a/solution.py
+++ b/solution.py
@@ -205,10 +205,11 @@
     from_z(order[-1])
     c_copy[0].wait_recv()
     c_copy[1].wait_recv()
-    quad(0)
     for s in order:
         from_x(s)
         from_y(s)
+        if s == order[0]:
+            quad(0)
     for s in order[:-1]:
         from_far(s)
     finish(order[0])

time: 23 us -> 23 us (level)
  no operation moved by 1% of the time
where the time goes in v4:
time: 23 us; the launch traced here: 22.9 us
  Pallas kernels  21.5 us (93%)
  local copies, waits for them, and re-layouts  0.66 us (3%)
  between operations  0.66 us (3%)
    pallas_call x1, Pallas kernels, on_device(): pl.pallas_call(functools.partial(ring_kernel, parts), out_shape=out_shape...  21.5 us
    unnamed x1, local copies, waits for them, and re-layouts  0.66 us

profile of v4, /device:TPU:0, one launch (start us, length us, event | category | flops | bytes accessed | tf_op | source)
XLA Modules:
  0.0 22.9 jit_solution(1372784617950040944)
XLA Ops:
  0.7 21.5 %shard_map.73 = bf16[1,16,4096]{2,1,0:T(8,128)(2,1)S(1)} custom-call(s32[1]{0:T(128)S(6)} %copy.10.counts_ref, bf16[128,4096]{1,0:T(8,128)(2,1)} %cot_ref.1, bf16[1024,768]{1,0:T(8,128)(2,1)} %bitcast.4, bf16[8,128]{1,0:T(8,128)(2,1)} %bitcast.7, s32[8,128]{1,0:T(8,128)} %bitcast.6, bf16[64,4096]{1,0:T(8,128)(2,1)} %out_basis_ref.1, bf16[64,768]{1,0:T(8,128)(2,1)} %bitcast.5), custom_call_target="tpu_custom_call" | custom-call | flops 1744830464 | bytes 4194304 | tf_op jit(solution)/shard_map/pallas_call | solution.py:289
  22.2 0.7 %copy.9 = bf16[1,16,4096]{2,1,0:T(8,128)(2,1)} copy(bf16[1,16,4096]{2,1,0:T(8,128)(2,1)S(1)} %shard_map.73) | data formatting | bytes 262144
